TPU v7x, 128 devices: a whole 4x4x4 slice. The times are simulated.
128 devices in a mesh: gx: 16 (over z_lo, x, core), gy: 8 (over z_hi, y).
Axes of the slice: x: 4, y: 4, z: 4 (z_hi: 2, z_lo: 2; z = z_hi * 2 + z_lo), core: 2. Of those that a mesh axis runs over, the one named last changes fastest.
Arguments:
- adjoint_in: float32 [4, 72, 512, 1024], P(None, None, 'gx', 'gy'), may hold values from -6 to 6
- courant_x: float32 [72, 512, 1024], P(None, 'gx', 'gy'), may hold values from -0.9 to 0.9
- courant_y: float32 [72, 512, 1024], P(None, 'gx', 'gy'), may hold values from -0.9 to 0.9
- mixing: float32 [71, 512, 1024], P(None, 'gx', 'gy'), may hold values from 0.05 to 5
- kernel_rows: bfloat16 [72, 524288], P(None, ('gx', 'gy')), may hold values from -6 to 6
- tracer_weights: bfloat16 [4, 524288], P(None, ('gx', 'gy')), may hold values from 0.25 to 1.5
- column_ids: int32 [524288], P(('gx', 'gy')), may hold values from 0 to 4095
- counts: int32 [128, 128], P(('gx', 'gy')), may hold values from 0 to 32, as said below
Outputs:
- adjoint_out: float32 [4, 72, 512, 1024], P(None, None, 'gx', 'gy')
- flux_gradient: float32 [4, 512, 1024], P(None, 'gx', 'gy')
Inputs may be any that keep to these rules, and one draw needn't show every extreme that they name: `counts`: live slots from one device to another; 32 is reached by one receiving device from every sender. `column_ids`: column id in the receiving tile, longitude-major.
All inputs are finite; a program needn't handle non-finite values.
Results may differ from a plain program's by a relative error of at most 0.0003.
Values may be sent and summed in bfloat16 or wider, within the bound.
No kernel may reach another device: no remote copies, remote signals or barrier semaphores. Data moves between devices by JAX's collectives and lax.ppermute only.
A program may use at most 320 MiB of HBM per device.

v0:
```python
import jax
import jax.numpy as jnp
from jax import lax
from jax.sharding import PartitionSpec as P

STEPS = 2
first_coef = (0.75, -0.15, 1.0 / 60.0)
second_coef = (1.5, -0.15, 1.0 / 90.0)
second_center = -49.0 / 18.0


def extended(cells, sides, width, closed):
    for axis, dim in sides:
        count = lax.axis_size(axis)
        ends = count if closed else count - 1
        head = lax.slice_in_dim(cells, 0, width, axis=dim)
        tail = lax.slice_in_dim(cells, cells.shape[dim] - width, cells.shape[dim], axis=dim)
        cells = jnp.concatenate(
            [
                lax.ppermute(tail, axis, [(i, (i + 1) % count) for i in range(ends)]),
                cells,
                lax.ppermute(head, axis, [((i + 1) % count, i) for i in range(ends)]),
            ],
            axis=dim,
        )
    return cells


def advect(padded, courant, axis, length):

    def piece(offset):
        return lax.slice_in_dim(padded, 3 + offset, 3 + offset + length, axis=axis)

    center = piece(0)
    slope = first_coef[0] * (piece(1) - piece(-1))
    curve = second_center * center + second_coef[0] * (piece(1) + piece(-1))
    for shift_k in (2, 3):
        slope = slope + first_coef[shift_k - 1] * (piece(shift_k) - piece(-shift_k))
        curve = curve + second_coef[shift_k - 1] * (piece(shift_k) + piece(-shift_k))
    return center + courant * slope + 0.5 * courant * courant * curve


def factor(mixing):
    levels = mixing.shape[0] + 1
    cps = []
    invs = []
    for level in range(levels):
        diag_part = jnp.ones_like(mixing[0])
        if level > 0:
            diag_part = diag_part + mixing[level - 1]
        if level < levels - 1:
            diag_part = diag_part + mixing[level]
        if level > 0:
            diag_part = diag_part - mixing[level - 1] * cps[level - 1] * -1.0
        inverse = 1.0 / diag_part
        invs.append(inverse)
        if level < levels - 1:
            cps.append(-mixing[level] * inverse)
    return (cps, invs)


def solve(field, mixing, cps, invs):
    levels = len(invs)
    carry = field[..., 0, :, :] * invs[0]
    forward = [carry]
    for level in range(1, levels):
        carry = (field[..., level, :, :] + mixing[level - 1] * carry) * invs[level]
        forward.append(carry)
    result = [None] * levels
    result[levels - 1] = forward[levels - 1]
    for level in range(levels - 2, -1, -1):
        result[level] = forward[level] - cps[level] * result[level + 1]
    return jnp.stack(result, axis=-3)


def local(
    adjoint_in, courant_x, courant_y, mixing, kernel_rows, tracer_weights, column_ids, counts
):
    tracer_count, level_count, lon_cells, lat_cells = adjoint_in.shape
    devices = lax.axis_size(("gx", "gy"))
    slot_count = kernel_rows.shape[1] // devices
    slot_place = jnp.arange(devices * slot_count, dtype=jnp.int32) % slot_count
    limits = jnp.repeat(counts[0], slot_count, total_repeat_length=devices * slot_count)
    live_rows = jnp.where((slot_place < limits)[None, :], kernel_rows, jnp.zeros_like(kernel_rows))
    got_rows, got_weights = (
        lax.all_to_all(live_rows, ("gx", "gy"), split_axis=1, concat_axis=1, tiled=True),
        lax.all_to_all(tracer_weights, ("gx", "gy"), split_axis=1, concat_axis=1, tiled=True),
    )
    cell_range = jnp.arange(lon_cells * lat_cells, dtype=jnp.int32)
    onehot = (column_ids[:, None] == cell_range[None, :]).astype(jnp.bfloat16)
    forcing_list = []
    for tracer in range(tracer_count):
        placed = onehot * got_weights[tracer][:, None]
        forcing_list.append(jnp.dot(got_rows, placed, preferred_element_type=jnp.float32))
    forcing = jnp.stack(forcing_list, axis=0)
    state = adjoint_in + forcing.reshape(tracer_count, level_count, lon_cells, lat_cells)
    cps, invs = factor(mixing)
    gradient = jnp.zeros((tracer_count, lon_cells, lat_cells), jnp.float32)
    for step in range(STEPS):
        wrapped = extended(state, (("gx", 2),), 3, True)
        zonal = advect(wrapped, courant_x, 2, lon_cells)
        padded = extended(zonal, (("gy", 3),), 3, False)
        meridional = advect(padded, courant_y, 3, lat_cells)
        state = solve(meridional, mixing, cps, invs)
        gradient = gradient + state[:, 0]
    return (state, gradient)


def solution(mesh):
    in_specs = (
        P(None, None, "gx", "gy"),
        P(None, "gx", "gy"),
        P(None, "gx", "gy"),
        P(None, "gx", "gy"),
        P(None, ("gx", "gy")),
        P(None, ("gx", "gy")),
        P(("gx", "gy")),
        P(("gx", "gy"), None),
    )
    out_specs = (P(None, None, "gx", "gy"), P(None, "gx", "gy"))
    return jax.shard_map(local, mesh=mesh, in_specs=in_specs, out_specs=out_specs, check_vma=False)
```

profile of v0, /device:TPU:64, one launch (start us, length us, event | category | flops | bytes accessed | tf_op | source)
XLA Modules:
  0.0 418.8 jit_solution(15522353103420576083)
XLA Ops:
  2.3 10.0 %all-to-all-start.1 = ((bf16[4,128,32]{2,0,1:T(4,128)(2,1)}), bf16[4,128,32]{2,0,1:T(4,128)(2,1)S(1)}, u32[]{:S(2)}, u32[]{:S(2)}) async-start(bf16[4,128,32]{2,0,1:T(4,128)(2,1)} %copy.1397), calls=%async_computation.1 | async-start | bytes 262144 | tf_op jit(solution)/shard_map/all_to_all | solution.py:87
  17.0 24.7 %gather_fusion = s32[4096]{0:T(1024)S(1)} fusion(s32[128]{0:T(128)S(1)} %bitcast.3716, s32[4096]{0:T(1024)S(1)} %broadcast_clamp_fusion), kind=kCustom, calls=%fused_computation | custom fusion | bytes 49152 | tf_op jit(solution)/shard_map/jit(_take)/gather | solution.py:83
  66.1 10.6 %all-to-all-start = ((bf16[72,128,32]{0,2,1:T(8,128)(2,1)}), bf16[72,128,32]{0,2,1:T(8,128)(2,1)}, u32[]{:S(2)}, u32[]{:S(2)}) async-start(bf16[72,128,32]{0,2,1:T(8,128)(2,1)} %bitcast.6), calls=%async_computation | async-start | bytes 2097152 | tf_op jit(solution)/shard_map/all_to_all | solution.py:86
  86.3 7.5 %all-to-all-done = bf16[72,128,32]{0,2,1:T(8,128)(2,1)} async-done(((bf16[72,128,32]{0,2,1:T(8,128)(2,1)}), bf16[72,128,32]{0,2,1:T(8,128)(2,1)}, u32[]{:S(2)}, u32[]{:S(2)}) %all-to-all-start) | async-done | bytes 589856 | tf_op jit(solution)/shard_map/all_to_all | solution.py:86
  93.8 13.3 %fusion.3 = f32[72,32,128]{2,0,1:T(8,128)S(1)} fusion(bf16[72,4096,1]{0,1,2:T(8,128)(2,1)} %bitcast.8, s32[32,128]{1,0:T(8,128)} %multiply_add_fusion.4, s32[4096]{0:T(1024)} %param.16, bf16[4096]{0:T(1024)(128)(2,1)} %mul.20172), kind=kOutput, calls=%fused_computation.8 | convolution fusion | flops 2449473536 | bytes 1810432 | tf_op jit(solution)/shard_map/dot_general | solution.py:94
  107.2 13.1 %fusion.2 = f32[72,32,128]{2,0,1:T(8,128)S(1)} fusion(bf16[72,4096,1]{0,1,2:T(8,128)(2,1)} %bitcast.8, s32[32,128]{1,0:T(8,128)S(1)} %copy-done.212, s32[4096]{0:T(1024)S(1)} %copy-done.216, bf16[4096]{0:T(1024)(128)(2,1)S(1)} %copy-done.213), kind=kOutput, calls=%fused_computation.7 | convolution fusion | flops 2449473536 | bytes 1810432 | tf_op jit(solution)/shard_map/dot_general | solution.py:94
  120.3 13.3 %fusion.1 = f32[72,32,128]{2,0,1:T(8,128)S(1)} fusion(bf16[72,4096,1]{0,1,2:T(8,128)(2,1)} %bitcast.8, s32[32,128]{1,0:T(8,128)S(1)} %copy-done.212, s32[4096]{0:T(1024)S(1)} %copy-done.216, bf16[4096]{0:T(1024)(128)(2,1)S(1)} %copy-done.214), kind=kOutput, calls=%fused_computation.6 | convolution fusion | flops 2449473536 | bytes 1810432 | tf_op jit(solution)/shard_map/dot_general | solution.py:94
  133.6 13.2 %fusion = f32[72,32,128]{2,0,1:T(8,128)S(1)} fusion(bf16[72,4096,1]{0,1,2:T(8,128)(2,1)} %bitcast.8, s32[32,128]{1,0:T(8,128)S(1)} %copy-done.212, s32[4096]{0:T(1024)S(1)} %copy-done.216, bf16[4096]{0:T(1024)(128)(2,1)S(1)} %mul.20163), kind=kOutput, calls=%fused_computation.5 | convolution fusion | flops 2449473536 | bytes 1810432 | tf_op jit(solution)/shard_map/dot_general | solution.py:94
  152.9 3.7 collective-permute-done
  156.8 4.1 collective-permute-done.1
  161.0 6.4 %multiply_add_fusion.3 = f32[4,72,32,128]{3,2,0,1:T(8,128)S(1)} fusion(f32[4,72,32,128]{3,2,0,1:T(8,128)S(1)} %maximum_add_fusion, f32[4,72,3,128]{3,2,0,1:T(4,128)S(1)} %copy.1408, f32[4,72,3,128]{3,2,0,1:T(4,128)S(1)} %copy.1410, f32[72,32,128]{2,1,0:T(8,128)S(1)} %multiply_multiply_fusion.1, f32[72,32,128]{2,1,0:T(8,128)S(1)} %copy-done.6), kind=kLoop, calls=%fused_computation.94 | loop fusion | flops 33030144 | bytes 12681216 | tf_op jit(solution)/shard_map/add | solution.py:40
  167.5 5.4 %fusion.559 = (f32[4,72,32,3]{3,2,0,1:T(8,128)}, f32[4,72,32,3]{3,2,0,1:T(8,128)}) fusion(f32[4,72,32,128]{3,2,0,1:T(8,128)S(1)} %multiply_add_fusion.3), kind=kLoop, calls=%fused_computation.1324 | loop fusion | bytes 442368 | tf_op jit(solution)/shard_map/slice | solution.py:17
  172.8 4.1 copy.1413
  176.9 4.0 copy.1411
  187.2 8.2 %collective-permute-done.3 = f32[4,72,32,3]{1,2,3,0:T(8,128)S(1)} collective-permute-done((f32[4,72,32,3]{1,2,3,0:T(8,128)S(1)}, f32[4,72,32,3]{1,2,3,0:T(8,128)S(1)}, u32[]{:S(2)}, u32[]{:S(2)}) %collective-permute-start.3) | collective-permute-done | bytes 110624 | tf_op jit(solution)/shard_map/ppermute | solution.py:20
  195.4 5.0 %copy.1414 = f32[4,72,32,3]{3,2,0,1:T(8,128)} copy(f32[4,72,32,3]{1,2,3,0:T(8,128)S(1)} %collective-permute-done.3) | data formatting | bytes 221184 | tf_op jit(solution)/shard_map/ppermute | solution.py:20
  200.4 5.1 %copy.1412 = f32[4,72,32,3]{3,2,0,1:T(8,128)} copy(f32[4,72,32,3]{1,2,3,0:T(8,128)S(1)} %collective-permute-done.2) | data formatting | bytes 221184 | tf_op jit(solution)/shard_map/ppermute | solution.py:22
  205.8 32.6 %multiply_add_fusion.2 = f32[4,72,32,128]{3,2,0,1:T(8,128)S(1)} fusion(f32[4,72,32,128]{3,2,0,1:T(8,128)} %copy-done.3, f32[4,72,32,3]{3,2,0,1:T(8,128)} %copy.1412, f32[4,72,32,3]{3,2,0,1:T(8,128)} %copy.1414, f32[72,32,128]{2,1,0:T(8,128)S(1)} %copy-done.11, f32[72,32,128]{2,1,0:T(8,128)S(1)} %copy-done.9), kind=kLoop, calls=%fused_computation.93 | loop fusion | flops 33030144 | bytes 12017664 | tf_op jit(solution)/shard_map/add | solution.py:40
  241.0 3.9 constant_dynamic-update-slice_fusion.71
  263.9 6.9 %collective-permute-done.5 = f32[4,72,3,128]{3,1,2,0:T(8,128)S(1)} collective-permute-done((f32[4,72,3,128]{3,1,2,0:T(8,128)S(1)}, f32[4,72,3,128]{3,1,2,0:T(8,128)S(1)}, u32[]{:S(2)}, u32[]{:S(2)}) %collective-permute-start.5) | collective-permute-done | bytes 442400 | tf_op jit(solution)/shard_map/ppermute | solution.py:20
  271.2 22.3 %add_multiply_fusion.5 = (f32[4,72,32,128]{3,2,0,1:T(8,128)}, f32[4,72,32,128]{3,2,0,1:T(8,128)}, f32[4,72,32,128]{3,2,0,1:T(8,128)}, f32[4,72,32,128]{3,2,0,1:T(8,128)}) fusion(f32[4,72,35,128]{3,2,0,1:T(8,128)S(1)} %copy_dynamic-update-slice_fusion, f32[4,72,32,128]{3,2,0,1:T(8,128)} %get-tuple-element.305, f32[4,72,3,128]{3,2,0,1:T(4,128)S(1)} %copy.1522, ...), kind=kLoop, calls=%fused_computation.91 | loop fusion | flops 24772608 | bytes 39370752 | tf_op jit(solution)/shard_map/mul | solution.py:36
  293.5 9.6 %copy_add_fusion.4 = f32[4,72,32,128]{3,2,1,0:T(8,128)S(1)} fusion(f32[4,72,32,128]{3,2,0,1:T(8,128)} %get-tuple-element.298, f32[4,72,32,128]{3,2,0,1:T(8,128)} %get-tuple-element.297, f32[4,72,32,128]{3,2,0,1:T(8,128)} %get-tuple-element.299, f32[4,72,32,128]{3,2,0,1:T(8,128)} %get-tuple-element.296, f32[4,72,32,128]{3,2,1,0:T(8,128)} %copy-done.4, ...), kind=kLoop, calls=%fused_computation.80 | loop fusion | flops 7077888 | bytes 29491200 | tf_op jit(solution)/shard_map/add | solution.py:40
  303.1 5.4 %fusion.557 = (f32[4,72,32,3]{3,2,1,0:T(8,128)}, f32[4,72,32,3]{3,2,1,0:T(8,128)}) fusion(f32[4,72,32,128]{3,2,1,0:T(8,128)S(1)} %copy_add_fusion.4), kind=kLoop, calls=%fused_computation.1322 | loop fusion | bytes 442368 | tf_op jit(solution)/shard_map/slice | solution.py:17
  308.5 4.0 copy.1534
  314.4 4.0 copy.1531
  318.4 7.5 %collective-permute-start.6 = (f32[4,72,32,3]{1,2,3,0:T(8,128)S(1)}, f32[4,72,32,3]{1,2,3,0:T(8,128)S(1)}, u32[]{:S(2)}, u32[]{:S(2)}) collective-permute-start(f32[4,72,32,3]{1,2,3,0:T(8,128)S(1)} %copy.1531), channel_id=1, source_target_pairs={{1,0},{2,1},{3,2},{4,3},{5,4},{6,5},{7,6},{9,8},{10,9},{11,10},{12... | collective-permute-start | bytes 331784 | tf_op jit(solution)/shard_map/ppermute | solution.py:22
  325.9 5.2 %copy.1537 = f32[4,72,32,128]{3,2,0,1:T(8,128)} copy(f32[4,72,32,128]{3,2,1,0:T(8,128)} %copy-done.2) | data formatting | bytes 9437184 | tf_op jit(solution)/shard_map/add | solution.py:40
  331.2 5.2 %copy.1535 = f32[4,72,32,3]{3,2,0,1:T(8,128)} copy(f32[4,72,32,3]{1,2,3,0:T(8,128)S(1)} %collective-permute-done.7) | data formatting | bytes 221184 | tf_op jit(solution)/shard_map/ppermute | solution.py:20
  336.4 4.9 %copy.1533 = f32[4,72,32,3]{3,2,0,1:T(8,128)} copy(f32[4,72,32,3]{1,2,3,0:T(8,128)S(1)} %collective-permute-done.6) | data formatting | bytes 221184 | tf_op jit(solution)/shard_map/ppermute | solution.py:22
  341.4 45.7 %add_multiply_fusion.2 = (f32[4,72,32,128]{3,2,0,1:T(8,128)}, f32[4,72,32,128]{3,2,0,1:T(8,128)}, f32[4,72,32,128]{3,2,0,1:T(8,128)}) fusion(f32[4,72,32,3]{3,2,0,1:T(8,128)} %copy.1533, f32[4,72,32,128]{3,2,0,1:T(8,128)} %copy.1537, f32[4,72,32,3]{3,2,0,1:T(8,128)} %copy.1535, f32[72,32,128]{2,1,0:T(8,128)S(1)} %copy-done.10), kind=kLoop, calls=%fused_computation.87 | loop fusion | flops 25952256 | bytes 20275200 | tf_op jit(solution)/shard_map/mul | solution.py:36
  387.4 11.0 %copy_add_fusion = f32[4,72,32,128]{3,2,1,0:T(8,128)S(1)} fusion(f32[4,72,32,128]{3,2,0,1:T(8,128)} %get-tuple-element.294, f32[4,72,32,128]{3,2,0,1:T(8,128)} %get-tuple-element.295, f32[4,72,32,128]{3,2,0,1:T(8,128)} %get-tuple-element.293, f32[4,72,32,128]{3,2,1,0:T(8,128)S(1)} %bitcast.3718, f32[72,32,128]{2,1,0:T(8,128)S(1)} %copy-done.12, ...), kind=kLoop, calls=%fused_computation.75 | loop fusion | flops 11796480 | bytes 29712384 | tf_op jit(solution)/shard_map/add | solution.py:40
  400.8 4.5 %fusion.442 = (f32[4,32,128]{2,1,0:T(8,128)}, f32[4,32,128]{2,1,0:T(8,128)S(1)}, f32[4,32,128]{2,1,0:T(8,128)S(1)}, f32[4,32,128]{2,1,0:T(8,128)S(1)}, f32[4,32,...) fusion(f32[4,32,128]{2,1,0:T(8,128)} %get-tuple-element.140, ...), kind=kLoop, calls=%fused_computation.1321 | loop fusion | flops 5210112 | bytes 10092544 | tf_op jit(solution)/shard_map/add | solution.py:105
  (672 shorter events, 89.2 us)
Async XLA Ops:
  2.3 63.8 %all-to-all-start.1 = ((bf16[4,128,32]{2,0,1:T(4,128)(2,1)}), bf16[4,128,32]{2,0,1:T(4,128)(2,1)S(1)}, u32[]{:S(2)}, u32[]{:S(2)}) async-start(bf16[4,128,32]{2,0,1:T(4,128)(2,1)} %copy.1397), calls=%async_computation.1 | async-start | bytes 262144 | tf_op jit(solution)/shard_map/all_to_all | solution.py:87
  16.2 42.6 %copy-start.50 = (f32[32,128]{1,0:T(8,128)}, f32[32,128]{1,0:T(8,128)S(1)}, u32[]{:S(2)}) copy-start(f32[32,128]{1,0:T(8,128)S(1)} %get-tuple-element.201) | copy-start | bytes 49156
  66.1 27.7 %all-to-all-start = ((bf16[72,128,32]{0,2,1:T(8,128)(2,1)}), bf16[72,128,32]{0,2,1:T(8,128)(2,1)}, u32[]{:S(2)}, u32[]{:S(2)}) async-start(bf16[72,128,32]{0,2,1:T(8,128)(2,1)} %bitcast.6), calls=%async_computation | async-start | bytes 2097152 | tf_op jit(solution)/shard_map/all_to_all | solution.py:86
  78.1 82.9 %copy-start.7 = (f32[72,32,128]{2,1,0:T(8,128)}, f32[72,32,128]{2,1,0:T(8,128)S(1)}, u32[]{:S(2)}) copy-start(f32[72,32,128]{2,1,0:T(8,128)S(1)} %multiply_multiply_fusion.1) | copy-start | bytes 3538948
  149.5 7.1 %collective-permute-start = (f32[4,72,3,128]{3,1,2,0:T(8,128)S(1)}, f32[4,72,3,128]{3,1,2,0:T(8,128)S(1)}, u32[]{:S(2)}, u32[]{:S(2)}) collective-permute-start(f32[4,72,3,128]{3,1,2,0:T(8,128)S(1)} %copy.1407), channel_id=1, source_target_pairs={{8,0},{16,8},{24,16},{32,24},{40,32},{48,40},{56,48},{64,56},{72,6... | collective-permute-start | bytes 1327112 | tf_op jit(solution)/shard_map/ppermute | solution.py:22
  150.8 10.0 %collective-permute-start.1 = (f32[4,72,3,128]{3,1,2,0:T(8,128)S(1)}, f32[4,72,3,128]{3,1,2,0:T(8,128)S(1)}, u32[]{:S(2)}, u32[]{:S(2)}) collective-permute-start(f32[4,72,3,128]{3,1,2,0:T(8,128)S(1)} %copy.1409), channel_id=1, source_target_pairs={{0,8},{8,16},{16,24},{24,32},{32,40},{40,48},{48,56},{56,64},{64,7... | collective-permute-start | bytes 1327112 | tf_op jit(solution)/shard_map/ppermute | solution.py:20
  180.9 19.5 %collective-permute-start.2 = (f32[4,72,32,3]{1,2,3,0:T(8,128)S(1)}, f32[4,72,32,3]{1,2,3,0:T(8,128)S(1)}, u32[]{:S(2)}, u32[]{:S(2)}) collective-permute-start(f32[4,72,32,3]{1,2,3,0:T(8,128)S(1)} %copy.1411), channel_id=1, source_target_pairs={{1,0},{2,1},{3,2},{4,3},{5,4},{6,5},{7,6},{9,8},{10,9},{11,10},{12... | collective-permute-start | bytes 331784 | tf_op jit(solution)/shard_map/ppermute | solution.py:22
  184.2 11.2 %collective-permute-start.3 = (f32[4,72,32,3]{1,2,3,0:T(8,128)S(1)}, f32[4,72,32,3]{1,2,3,0:T(8,128)S(1)}, u32[]{:S(2)}, u32[]{:S(2)}) collective-permute-start(f32[4,72,32,3]{1,2,3,0:T(8,128)S(1)} %copy.1413), channel_id=1, source_target_pairs={{0,1},{1,2},{2,3},{3,4},{4,5},{5,6},{6,7},{8,9},{9,10},{10,11},{11... | collective-permute-start | bytes 331784 | tf_op jit(solution)/shard_map/ppermute | solution.py:20
  187.1 51.3 %copy-start.204 = (f32[32,128]{1,0:T(8,128)}, f32[32,128]{1,0:T(8,128)S(1)}, u32[]{:S(2)}) copy-start(f32[32,128]{1,0:T(8,128)S(1)} %get-tuple-element.503) | copy-start | bytes 49156
  187.1 53.5 %copy-start.192 = (f32[32,128]{1,0:T(8,128)}, f32[32,128]{1,0:T(8,128)S(1)}, u32[]{:S(2)}) copy-start(f32[32,128]{1,0:T(8,128)S(1)} %get-tuple-element.504) | copy-start | bytes 49156
  187.1 53.5 %copy-start.202 = (f32[32,128]{1,0:T(8,128)}, f32[32,128]{1,0:T(8,128)S(1)}, u32[]{:S(2)}) copy-start(f32[32,128]{1,0:T(8,128)S(1)} %get-tuple-element.356) | copy-start | bytes 49156
  187.1 53.5 %copy-start.203 = (f32[32,128]{1,0:T(8,128)}, f32[32,128]{1,0:T(8,128)S(1)}, u32[]{:S(2)}) copy-start(f32[32,128]{1,0:T(8,128)S(1)} %get-tuple-element.502) | copy-start | bytes 49156
  187.1 60.7 %copy-start.135 = (f32[32,128]{1,0:T(8,128)}, f32[32,128]{1,0:T(8,128)S(1)}, u32[]{:S(2)}) copy-start(f32[32,128]{1,0:T(8,128)S(1)} %get-tuple-element.357) | copy-start | bytes 49156
  187.1 60.7 %copy-start.137 = (f32[32,128]{1,0:T(8,128)}, f32[32,128]{1,0:T(8,128)S(1)}, u32[]{:S(2)}) copy-start(f32[32,128]{1,0:T(8,128)S(1)} %get-tuple-element.501) | copy-start | bytes 49156
  205.5 33.0 %copy-start.19 = (f32[1,32,128]{2,1,0:T(8,128)S(1)}, f32[1,32,128]{2,1,0:T(8,128)}, u32[]{:S(2)}) copy-start(f32[1,32,128]{2,1,0:T(8,128)} %copy-done.18) | copy-start | bytes 49156
  205.5 33.0 %copy-start.21 = (f32[1,32,128]{2,1,0:T(8,128)S(1)}, f32[1,32,128]{2,1,0:T(8,128)}, u32[]{:S(2)}) copy-start(f32[1,32,128]{2,1,0:T(8,128)} %copy-done.20) | copy-start | bytes 49156
  205.5 33.0 %copy-start.23 = (f32[1,32,128]{2,1,0:T(8,128)S(1)}, f32[1,32,128]{2,1,0:T(8,128)}, u32[]{:S(2)}) copy-start(f32[1,32,128]{2,1,0:T(8,128)} %copy-done.22) | copy-start | bytes 49156
  205.5 33.0 %copy-start.25 = (f32[1,32,128]{2,1,0:T(8,128)S(1)}, f32[1,32,128]{2,1,0:T(8,128)}, u32[]{:S(2)}) copy-start(f32[1,32,128]{2,1,0:T(8,128)} %copy-done.24) | copy-start | bytes 49156
  205.5 33.0 %copy-start.27 = (f32[1,32,128]{2,1,0:T(8,128)S(1)}, f32[1,32,128]{2,1,0:T(8,128)}, u32[]{:S(2)}) copy-start(f32[1,32,128]{2,1,0:T(8,128)} %copy-done.26) | copy-start | bytes 49156
  205.5 33.0 %copy-start.29 = (f32[1,32,128]{2,1,0:T(8,128)S(1)}, f32[1,32,128]{2,1,0:T(8,128)}, u32[]{:S(2)}) copy-start(f32[1,32,128]{2,1,0:T(8,128)} %copy-done.28) | copy-start | bytes 49156
  205.5 33.0 %copy-start.31 = (f32[1,32,128]{2,1,0:T(8,128)S(1)}, f32[1,32,128]{2,1,0:T(8,128)}, u32[]{:S(2)}) copy-start(f32[1,32,128]{2,1,0:T(8,128)} %copy-done.30) | copy-start | bytes 49156
  205.6 33.0 %copy-start.33 = (f32[1,32,128]{2,1,0:T(8,128)S(1)}, f32[1,32,128]{2,1,0:T(8,128)}, u32[]{:S(2)}) copy-start(f32[1,32,128]{2,1,0:T(8,128)} %copy-done.32) | copy-start | bytes 49156
  205.6 33.0 %copy-start.35 = (f32[1,32,128]{2,1,0:T(8,128)S(1)}, f32[1,32,128]{2,1,0:T(8,128)}, u32[]{:S(2)}) copy-start(f32[1,32,128]{2,1,0:T(8,128)} %copy-done.34) | copy-start | bytes 49156
  205.6 33.0 %copy-start.37 = (f32[1,32,128]{2,1,0:T(8,128)S(1)}, f32[1,32,128]{2,1,0:T(8,128)}, u32[]{:S(2)}) copy-start(f32[1,32,128]{2,1,0:T(8,128)} %copy-done.36) | copy-start | bytes 49156
  205.6 33.0 %copy-start.39 = (f32[1,32,128]{2,1,0:T(8,128)S(1)}, f32[1,32,128]{2,1,0:T(8,128)}, u32[]{:S(2)}) copy-start(f32[1,32,128]{2,1,0:T(8,128)} %copy-done.38) | copy-start | bytes 49156
  259.6 11.3 %collective-permute-start.4 = (f32[4,72,3,128]{3,1,2,0:T(8,128)S(1)}, f32[4,72,3,128]{3,1,2,0:T(8,128)S(1)}, u32[]{:S(2)}, u32[]{:S(2)}) collective-permute-start(f32[4,72,3,128]{3,1,2,0:T(8,128)S(1)} %copy.1518), channel_id=1, source_target_pairs={{8,0},{16,8},{24,16},{32,24},{40,32},{48,40},{56,48},{64,56},{72,6... | collective-permute-start | bytes 1327112 | tf_op jit(solution)/shard_map/ppermute | solution.py:22
  260.9 9.8 %collective-permute-start.5 = (f32[4,72,3,128]{3,1,2,0:T(8,128)S(1)}, f32[4,72,3,128]{3,1,2,0:T(8,128)S(1)}, u32[]{:S(2)}, u32[]{:S(2)}) collective-permute-start(f32[4,72,3,128]{3,1,2,0:T(8,128)S(1)} %copy.1521), channel_id=1, source_target_pairs={{0,8},{8,16},{16,24},{24,32},{32,40},{40,48},{48,56},{56,64},{64,7... | collective-permute-start | bytes 1327112 | tf_op jit(solution)/shard_map/ppermute | solution.py:20
  312.5 18.7 %collective-permute-start.7 = (f32[4,72,32,3]{1,2,3,0:T(8,128)S(1)}, f32[4,72,32,3]{1,2,3,0:T(8,128)S(1)}, u32[]{:S(2)}, u32[]{:S(2)}) collective-permute-start(f32[4,72,32,3]{1,2,3,0:T(8,128)S(1)} %copy.1534), channel_id=1, source_target_pairs={{0,1},{1,2},{2,3},{3,4},{4,5},{5,6},{6,7},{8,9},{9,10},{10,11},{11... | collective-permute-start | bytes 331784 | tf_op jit(solution)/shard_map/ppermute | solution.py:20
  318.4 18.0 %collective-permute-start.6 = (f32[4,72,32,3]{1,2,3,0:T(8,128)S(1)}, f32[4,72,32,3]{1,2,3,0:T(8,128)S(1)}, u32[]{:S(2)}, u32[]{:S(2)}) collective-permute-start(f32[4,72,32,3]{1,2,3,0:T(8,128)S(1)} %copy.1531), channel_id=1, source_target_pairs={{1,0},{2,1},{3,2},{4,3},{5,4},{6,5},{7,6},{9,8},{10,9},{11,10},{12... | collective-permute-start | bytes 331784 | tf_op jit(solution)/shard_map/ppermute | solution.py:22
  336.4 50.7 %slice-start = ((s8[4718592]{0:T(1024)(128)(4,1)}), s8[524288]{0:T(1024)(128)(4,1)S(1)}, s32[]{:S(2)}) async-start(s8[4718592]{0:T(1024)(128)(4,1)} %bitcast.3717), calls=%async_computation.2 | async-start | bytes 1048576
  341.3 45.7 %slice-start.1 = ((s8[4718592]{0:T(1024)(128)(4,1)}), s8[4194304]{0:T(1024)(128)(4,1)S(1)}, s32[]{:S(2)}) async-start(s8[4718592]{0:T(1024)(128)(4,1)} %bitcast.3717), calls=%async_computation.3 | async-start | bytes 8388608
  341.4 45.7 %copy-start.12 = (f32[72,32,128]{2,1,0:T(8,128)S(1)}, f32[72,32,128]{2,1,0:T(8,128)}, u32[]{:S(2)}) copy-start(f32[72,32,128]{2,1,0:T(8,128)} %multiply_multiply_fusion) | copy-start | bytes 3538948
  (199 other events, 2444.9 us)
where the time goes:
time: 425 us; the launch traced here: 419 us
  other arithmetic  194 us (46%)
  local copies, waits for them, and re-layouts  97.1 us (23%)
  matrix products  52.9 us (12%)
  starting transfers between devices  38.9 us (9%)
  waiting for transfers between devices  30.4 us (7%)
  between operations  5.31 us (1%)
    mul x2, other arithmetic, advect(): curve = second_center * center + second_coef[0] * (piece(1) + piece(-1))  68 us
    add x4, other arithmetic, advect(): return center + courant * slope + 0.5 * courant * courant * curve  59.5 us
    dot_general x4, matrix products, local(): jnp.dot(got_rows, placed, preferred_element_type=jnp.float32)  52.9 us
    unnamed x75, other arithmetic  27 us
    gather x1, local copies, waits for them, and re-layouts, local(): jnp.repeat(counts[0], slot_count, total_repeat_length=devices * slot_count)  24.7 us
    slice x8, local copies, waits for them, and re-layouts, extended(): lax.slice_in_dim(cells, cells.shape[dim] - width, cells.shape[dim], axis=...  19.4 us
    ppermute x4, waiting for transfers between devices, extended(): lax.ppermute(tail, axis, [(i, (i + 1) % count) for i in range(ends)])  19.1 us
    ppermute x4, starting transfers between devices, extended(): lax.ppermute(head, axis, [((i + 1) % count, i) for i in range(ends)])  13.4 us
  transfers between devices with their start and end apart: 10, of which 5 were waited for; matrix products, arithmetic and copies ran while one was open for 21% of the time, Pallas kernels for 0%

commit v1 on v0

--- a/solution.py
+++ b/solution.py
@@ -84,7 +84,15 @@
     live_rows = jnp.where((slot_place < limits)[None, :], kernel_rows, jnp.zeros_like(kernel_rows))
     got_rows, got_weights = (
         lax.all_to_all(live_rows, ("gx", "gy"), split_axis=1, concat_axis=1, tiled=True),
-        lax.all_to_all(tracer_weights, ("gx", "gy"), split_axis=1, concat_axis=1, tiled=True),
+        jnp.concatenate(
+            lax.all_to_all(
+                jnp.stack(jnp.split(tracer_weights, lax.axis_size(("gx", "gy")), axis=1)),
+                ("gx", "gy"),
+                0,
+                0,
+            ),
+            axis=1,
+        ),
     )
     cell_range = jnp.arange(lon_cells * lat_cells, dtype=jnp.int32)
     onehot = (column_ids[:, None] == cell_range[None, :]).astype(jnp.bfloat16)

time: 425 us -> 593 us (1.40)
  local copies, waits for them, and re-layouts: 97.1 us -> 262 us
    unnamed x512 -> x639, local copies, waits for them, and re-layouts: 6.58 us -> 172 us
  transfers between devices with their start and end apart: 10 -> 10, of which waited for: 5 -> 5; matrix products, arithmetic and copies ran while one was open for 21% -> 15% of each run, Pallas kernels for 0% -> 0%
where the time goes in v1:
time: 593 us; the launch traced here: 584 us
  local copies, waits for them, and re-layouts  262 us (44%)
  other arithmetic  194 us (33%)
  matrix products  52.9 us (9%)
  starting transfers between devices  38.9 us (7%)
  waiting for transfers between devices  30.4 us (5%)
    unnamed x639, local copies, waits for them, and re-layouts  172 us
    mul x2, other arithmetic, advect(): curve = second_center * center + second_coef[0] * (piece(1) + piece(-1))  68 us
    add x4, other arithmetic, advect(): return center + courant * slope + 0.5 * courant * courant * curve  59.5 us
    dot_general x4, matrix products, local(): jnp.dot(got_rows, placed, preferred_element_type=jnp.float32)  52.9 us
    unnamed x75, other arithmetic  27 us
    gather x1, local copies, waits for them, and re-layouts, local(): jnp.repeat(counts[0], slot_count, total_repeat_length=devices * slot_count)  24.7 us
    slice x8, local copies, waits for them, and re-layouts, extended(): lax.slice_in_dim(cells, cells.shape[dim] - width, cells.shape[dim], axis=...  19.4 us
    ppermute x4, waiting for transfers between devices, extended(): lax.ppermute(tail, axis, [(i, (i + 1) % count) for i in range(ends)])  19.1 us
  transfers between devices with their start and end apart: 10, of which 5 were waited for; matrix products, arithmetic and copies ran while one was open for 15% of the time, Pallas kernels for 0%

profile of v1, /device:TPU:64, one launch (start us, length us, event | category | flops | bytes accessed | tf_op | source)
XLA Modules:
  0.0 584.0 jit_solution(5589217764649513738)
XLA Ops:
  167.6 10.0 %all-to-all-start.1 = ((bf16[128,4,32]{2,1,0:T(4,128)(2,1)}), bf16[128,4,32]{2,1,0:T(4,128)(2,1)S(1)}, u32[]{:S(2)}, u32[]{:S(2)}) async-start(bf16[128,4,32]{2,1,0:T(4,128)(2,1)} %constant_dynamic-update-slice_fusion), calls=%async_computation.1 | async-start | bytes 262144 | tf_op jit(solution)/shard_map/all_to_all | solution.py:88
  182.3 24.7 %gather_fusion = s32[4096]{0:T(1024)S(1)} fusion(s32[128]{0:T(128)S(1)} %bitcast.3973, s32[4096]{0:T(1024)S(1)} %broadcast_clamp_fusion), kind=kCustom, calls=%fused_computation | custom fusion | bytes 49152 | tf_op jit(solution)/shard_map/jit(_take)/gather | solution.py:83
  231.3 10.6 %all-to-all-start = ((bf16[72,128,32]{0,2,1:T(8,128)(2,1)}), bf16[72,128,32]{0,2,1:T(8,128)(2,1)}, u32[]{:S(2)}, u32[]{:S(2)}) async-start(bf16[72,128,32]{0,2,1:T(8,128)(2,1)} %bitcast.6), calls=%async_computation | async-start | bytes 2097152 | tf_op jit(solution)/shard_map/all_to_all | solution.py:86
  251.5 7.5 %all-to-all-done = bf16[72,128,32]{0,2,1:T(8,128)(2,1)} async-done(((bf16[72,128,32]{0,2,1:T(8,128)(2,1)}), bf16[72,128,32]{0,2,1:T(8,128)(2,1)}, u32[]{:S(2)}, u32[]{:S(2)}) %all-to-all-start) | async-done | bytes 589856 | tf_op jit(solution)/shard_map/all_to_all | solution.py:86
  259.0 13.3 %fusion.3 = f32[72,32,128]{2,0,1:T(8,128)S(1)} fusion(bf16[72,4096,1]{0,1,2:T(8,128)(2,1)} %bitcast.8, s32[32,128]{1,0:T(8,128)} %multiply_add_fusion.4, s32[4096]{0:T(1024)} %param.16, bf16[4096]{0:T(1024)(128)(2,1)} %mul.20172), kind=kOutput, calls=%fused_computation.8 | convolution fusion | flops 2449473536 | bytes 1810432 | tf_op jit(solution)/shard_map/dot_general | solution.py:102
  272.4 13.1 %fusion.2 = f32[72,32,128]{2,0,1:T(8,128)S(1)} fusion(bf16[72,4096,1]{0,1,2:T(8,128)(2,1)} %bitcast.8, s32[32,128]{1,0:T(8,128)S(1)} %copy-done.212, s32[4096]{0:T(1024)S(1)} %copy-done.216, bf16[4096]{0:T(1024)(128)(2,1)S(1)} %copy-done.213), kind=kOutput, calls=%fused_computation.7 | convolution fusion | flops 2449473536 | bytes 1810432 | tf_op jit(solution)/shard_map/dot_general | solution.py:102
  285.5 13.3 %fusion.1 = f32[72,32,128]{2,0,1:T(8,128)S(1)} fusion(bf16[72,4096,1]{0,1,2:T(8,128)(2,1)} %bitcast.8, s32[32,128]{1,0:T(8,128)S(1)} %copy-done.212, s32[4096]{0:T(1024)S(1)} %copy-done.216, bf16[4096]{0:T(1024)(128)(2,1)S(1)} %copy-done.214), kind=kOutput, calls=%fused_computation.6 | convolution fusion | flops 2449473536 | bytes 1810432 | tf_op jit(solution)/shard_map/dot_general | solution.py:102
  298.9 13.2 %fusion = f32[72,32,128]{2,0,1:T(8,128)S(1)} fusion(bf16[72,4096,1]{0,1,2:T(8,128)(2,1)} %bitcast.8, s32[32,128]{1,0:T(8,128)S(1)} %copy-done.212, s32[4096]{0:T(1024)S(1)} %copy-done.216, bf16[4096]{0:T(1024)(128)(2,1)S(1)} %mul.20163), kind=kOutput, calls=%fused_computation.5 | convolution fusion | flops 2449473536 | bytes 1810432 | tf_op jit(solution)/shard_map/dot_general | solution.py:102
  318.2 3.7 collective-permute-done
  322.1 4.1 collective-permute-done.1
  326.3 6.4 %multiply_add_fusion.3 = f32[4,72,32,128]{3,2,0,1:T(8,128)S(1)} fusion(f32[4,72,32,128]{3,2,0,1:T(8,128)S(1)} %maximum_add_fusion, f32[4,72,3,128]{3,2,0,1:T(4,128)S(1)} %copy.2394, f32[4,72,3,128]{3,2,0,1:T(4,128)S(1)} %copy.2396, f32[72,32,128]{2,1,0:T(8,128)S(1)} %multiply_multiply_fusion.1, f32[72,32,128]{2,1,0:T(8,128)S(1)} %copy-done.6), kind=kLoop, calls=%fused_computation.94 | loop fusion | flops 33030144 | bytes 12681216 | tf_op jit(solution)/shard_map/add | solution.py:40
  332.7 5.4 fusion.559
  338.1 4.1 copy.2399
  342.1 4.0 copy.2397
  352.4 8.2 %collective-permute-done.3 = f32[4,72,32,3]{1,2,3,0:T(8,128)S(1)} collective-permute-done((f32[4,72,32,3]{1,2,3,0:T(8,128)S(1)}, f32[4,72,32,3]{1,2,3,0:T(8,128)S(1)}, u32[]{:S(2)}, u32[]{:S(2)}) %collective-permute-start.3) | collective-permute-done | bytes 110624 | tf_op jit(solution)/shard_map/ppermute | solution.py:20
  360.6 5.0 copy.2400
  365.6 5.1 copy.2398
  371.1 32.6 %multiply_add_fusion.2 = f32[4,72,32,128]{3,2,0,1:T(8,128)S(1)} fusion(f32[4,72,32,128]{3,2,0,1:T(8,128)} %copy-done.3, f32[4,72,32,3]{3,2,0,1:T(8,128)} %copy.2398, f32[4,72,32,3]{3,2,0,1:T(8,128)} %copy.2400, f32[72,32,128]{2,1,0:T(8,128)S(1)} %copy-done.11, f32[72,32,128]{2,1,0:T(8,128)S(1)} %copy-done.9), kind=kLoop, calls=%fused_computation.93 | loop fusion | flops 33030144 | bytes 12017664 | tf_op jit(solution)/shard_map/add | solution.py:40
  406.2 3.9 constant_dynamic-update-slice_fusion.199
  429.1 6.9 %collective-permute-done.5 = f32[4,72,3,128]{3,1,2,0:T(8,128)S(1)} collective-permute-done((f32[4,72,3,128]{3,1,2,0:T(8,128)S(1)}, f32[4,72,3,128]{3,1,2,0:T(8,128)S(1)}, u32[]{:S(2)}, u32[]{:S(2)}) %collective-permute-start.5) | collective-permute-done | bytes 442400 | tf_op jit(solution)/shard_map/ppermute | solution.py:20
  436.4 22.3 %add_multiply_fusion.5 = (f32[4,72,32,128]{3,2,0,1:T(8,128)}, f32[4,72,32,128]{3,2,0,1:T(8,128)}, f32[4,72,32,128]{3,2,0,1:T(8,128)}, f32[4,72,32,128]{3,2,0,1:T(8,128)}) fusion(f32[4,72,35,128]{3,2,0,1:T(8,128)S(1)} %copy_dynamic-update-slice_fusion, f32[4,72,32,128]{3,2,0,1:T(8,128)} %get-tuple-element.309, f32[4,72,3,128]{3,2,0,1:T(4,128)S(1)} %copy.2508, ...), kind=kLoop, calls=%fused_computation.91 | loop fusion | flops 24772608 | bytes 39370752 | tf_op jit(solution)/shard_map/mul | solution.py:36
  458.7 9.6 %copy_add_fusion.4 = f32[4,72,32,128]{3,2,1,0:T(8,128)S(1)} fusion(f32[4,72,32,128]{3,2,0,1:T(8,128)} %get-tuple-element.302, f32[4,72,32,128]{3,2,0,1:T(8,128)} %get-tuple-element.301, f32[4,72,32,128]{3,2,0,1:T(8,128)} %get-tuple-element.303, f32[4,72,32,128]{3,2,0,1:T(8,128)} %get-tuple-element.300, f32[4,72,32,128]{3,2,1,0:T(8,128)} %copy-done.4, ...), kind=kLoop, calls=%fused_computation.80 | loop fusion | flops 7077888 | bytes 29491200 | tf_op jit(solution)/shard_map/add | solution.py:40
  468.3 5.4 fusion.557
  473.7 4.0 copy.2520
  479.6 4.0 copy.2517
  483.6 7.5 %collective-permute-start.6 = (f32[4,72,32,3]{1,2,3,0:T(8,128)S(1)}, f32[4,72,32,3]{1,2,3,0:T(8,128)S(1)}, u32[]{:S(2)}, u32[]{:S(2)}) collective-permute-start(f32[4,72,32,3]{1,2,3,0:T(8,128)S(1)} %copy.2517), channel_id=1, source_target_pairs={{1,0},{2,1},{3,2},{4,3},{5,4},{6,5},{7,6},{9,8},{10,9},{11,10},{12... | collective-permute-start | bytes 331784 | tf_op jit(solution)/shard_map/ppermute | solution.py:22
  491.2 5.2 copy.2523
  496.4 5.2 copy.2521
  501.6 4.9 copy.2519
  506.6 45.7 %add_multiply_fusion.2 = (f32[4,72,32,128]{3,2,0,1:T(8,128)}, f32[4,72,32,128]{3,2,0,1:T(8,128)}, f32[4,72,32,128]{3,2,0,1:T(8,128)}) fusion(f32[4,72,32,3]{3,2,0,1:T(8,128)} %copy.2519, f32[4,72,32,128]{3,2,0,1:T(8,128)} %copy.2523, f32[4,72,32,3]{3,2,0,1:T(8,128)} %copy.2521, f32[72,32,128]{2,1,0:T(8,128)S(1)} %copy-done.10), kind=kLoop, calls=%fused_computation.87 | loop fusion | flops 25952256 | bytes 20275200 | tf_op jit(solution)/shard_map/mul | solution.py:36
  552.7 11.0 %copy_add_fusion = f32[4,72,32,128]{3,2,1,0:T(8,128)S(1)} fusion(f32[4,72,32,128]{3,2,0,1:T(8,128)} %get-tuple-element.298, f32[4,72,32,128]{3,2,0,1:T(8,128)} %get-tuple-element.299, f32[4,72,32,128]{3,2,0,1:T(8,128)} %get-tuple-element.297, f32[4,72,32,128]{3,2,1,0:T(8,128)S(1)} %bitcast.3975, f32[72,32,128]{2,1,0:T(8,128)S(1)} %copy-done.12, ...), kind=kLoop, calls=%fused_computation.75 | loop fusion | flops 11796480 | bytes 29712384 | tf_op jit(solution)/shard_map/add | solution.py:40
  566.1 4.5 fusion.442
  (798 shorter events, 254.3 us)
Async XLA Ops:
  0.6 181.6 %copy-start = (s32[1,128]{1,0:T(1,128)S(1)}, s32[1,128]{1,0:T(1,128)}, u32[]{:S(2)}) copy-start(s32[1,128]{1,0:T(1,128)} %param.17) | copy-start | bytes 1540
  167.6 63.8 %all-to-all-start.1 = ((bf16[128,4,32]{2,1,0:T(4,128)(2,1)}), bf16[128,4,32]{2,1,0:T(4,128)(2,1)S(1)}, u32[]{:S(2)}, u32[]{:S(2)}) async-start(bf16[128,4,32]{2,1,0:T(4,128)(2,1)} %constant_dynamic-update-slice_fusion), calls=%async_computation.1 | async-start | bytes 262144 | tf_op jit(solution)/shard_map/all_to_all | solution.py:88
  181.4 42.6 %copy-start.50 = (f32[32,128]{1,0:T(8,128)}, f32[32,128]{1,0:T(8,128)S(1)}, u32[]{:S(2)}) copy-start(f32[32,128]{1,0:T(8,128)S(1)} %get-tuple-element.205) | copy-start | bytes 49156
  231.3 27.7 %all-to-all-start = ((bf16[72,128,32]{0,2,1:T(8,128)(2,1)}), bf16[72,128,32]{0,2,1:T(8,128)(2,1)}, u32[]{:S(2)}, u32[]{:S(2)}) async-start(bf16[72,128,32]{0,2,1:T(8,128)(2,1)} %bitcast.6), calls=%async_computation | async-start | bytes 2097152 | tf_op jit(solution)/shard_map/all_to_all | solution.py:86
  243.3 82.9 %copy-start.7 = (f32[72,32,128]{2,1,0:T(8,128)}, f32[72,32,128]{2,1,0:T(8,128)S(1)}, u32[]{:S(2)}) copy-start(f32[72,32,128]{2,1,0:T(8,128)S(1)} %multiply_multiply_fusion.1) | copy-start | bytes 3538948
  314.8 7.1 %collective-permute-start = (f32[4,72,3,128]{3,1,2,0:T(8,128)S(1)}, f32[4,72,3,128]{3,1,2,0:T(8,128)S(1)}, u32[]{:S(2)}, u32[]{:S(2)}) collective-permute-start(f32[4,72,3,128]{3,1,2,0:T(8,128)S(1)} %copy.2393), channel_id=1, source_target_pairs={{8,0},{16,8},{24,16},{32,24},{40,32},{48,40},{56,48},{64,56},{72,6... | collective-permute-start | bytes 1327112 | tf_op jit(solution)/shard_map/ppermute | solution.py:22
  316.1 10.0 %collective-permute-start.1 = (f32[4,72,3,128]{3,1,2,0:T(8,128)S(1)}, f32[4,72,3,128]{3,1,2,0:T(8,128)S(1)}, u32[]{:S(2)}, u32[]{:S(2)}) collective-permute-start(f32[4,72,3,128]{3,1,2,0:T(8,128)S(1)} %copy.2395), channel_id=1, source_target_pairs={{0,8},{8,16},{16,24},{24,32},{32,40},{40,48},{48,56},{56,64},{64,7... | collective-permute-start | bytes 1327112 | tf_op jit(solution)/shard_map/ppermute | solution.py:20
  346.1 19.5 %collective-permute-start.2 = (f32[4,72,32,3]{1,2,3,0:T(8,128)S(1)}, f32[4,72,32,3]{1,2,3,0:T(8,128)S(1)}, u32[]{:S(2)}, u32[]{:S(2)}) collective-permute-start(f32[4,72,32,3]{1,2,3,0:T(8,128)S(1)} %copy.2397), channel_id=1, source_target_pairs={{1,0},{2,1},{3,2},{4,3},{5,4},{6,5},{7,6},{9,8},{10,9},{11,10},{12... | collective-permute-start | bytes 331784 | tf_op jit(solution)/shard_map/ppermute | solution.py:22
  349.4 11.2 %collective-permute-start.3 = (f32[4,72,32,3]{1,2,3,0:T(8,128)S(1)}, f32[4,72,32,3]{1,2,3,0:T(8,128)S(1)}, u32[]{:S(2)}, u32[]{:S(2)}) collective-permute-start(f32[4,72,32,3]{1,2,3,0:T(8,128)S(1)} %copy.2399), channel_id=1, source_target_pairs={{0,1},{1,2},{2,3},{3,4},{4,5},{5,6},{6,7},{8,9},{9,10},{10,11},{11... | collective-permute-start | bytes 331784 | tf_op jit(solution)/shard_map/ppermute | solution.py:20
  352.3 51.3 %copy-start.204 = (f32[32,128]{1,0:T(8,128)}, f32[32,128]{1,0:T(8,128)S(1)}, u32[]{:S(2)}) copy-start(f32[32,128]{1,0:T(8,128)S(1)} %get-tuple-element.507) | copy-start | bytes 49156
  352.3 53.5 %copy-start.192 = (f32[32,128]{1,0:T(8,128)}, f32[32,128]{1,0:T(8,128)S(1)}, u32[]{:S(2)}) copy-start(f32[32,128]{1,0:T(8,128)S(1)} %get-tuple-element.508) | copy-start | bytes 49156
  352.3 53.5 %copy-start.202 = (f32[32,128]{1,0:T(8,128)}, f32[32,128]{1,0:T(8,128)S(1)}, u32[]{:S(2)}) copy-start(f32[32,128]{1,0:T(8,128)S(1)} %get-tuple-element.360) | copy-start | bytes 49156
  352.3 53.5 %copy-start.203 = (f32[32,128]{1,0:T(8,128)}, f32[32,128]{1,0:T(8,128)S(1)}, u32[]{:S(2)}) copy-start(f32[32,128]{1,0:T(8,128)S(1)} %get-tuple-element.506) | copy-start | bytes 49156
  352.4 60.7 %copy-start.135 = (f32[32,128]{1,0:T(8,128)}, f32[32,128]{1,0:T(8,128)S(1)}, u32[]{:S(2)}) copy-start(f32[32,128]{1,0:T(8,128)S(1)} %get-tuple-element.361) | copy-start | bytes 49156
  352.4 60.7 %copy-start.137 = (f32[32,128]{1,0:T(8,128)}, f32[32,128]{1,0:T(8,128)S(1)}, u32[]{:S(2)}) copy-start(f32[32,128]{1,0:T(8,128)S(1)} %get-tuple-element.505) | copy-start | bytes 49156
  370.7 33.0 %copy-start.19 = (f32[1,32,128]{2,1,0:T(8,128)S(1)}, f32[1,32,128]{2,1,0:T(8,128)}, u32[]{:S(2)}) copy-start(f32[1,32,128]{2,1,0:T(8,128)} %copy-done.18) | copy-start | bytes 49156
  370.7 33.0 %copy-start.21 = (f32[1,32,128]{2,1,0:T(8,128)S(1)}, f32[1,32,128]{2,1,0:T(8,128)}, u32[]{:S(2)}) copy-start(f32[1,32,128]{2,1,0:T(8,128)} %copy-done.20) | copy-start | bytes 49156
  370.7 33.0 %copy-start.23 = (f32[1,32,128]{2,1,0:T(8,128)S(1)}, f32[1,32,128]{2,1,0:T(8,128)}, u32[]{:S(2)}) copy-start(f32[1,32,128]{2,1,0:T(8,128)} %copy-done.22) | copy-start | bytes 49156
  370.7 33.0 %copy-start.25 = (f32[1,32,128]{2,1,0:T(8,128)S(1)}, f32[1,32,128]{2,1,0:T(8,128)}, u32[]{:S(2)}) copy-start(f32[1,32,128]{2,1,0:T(8,128)} %copy-done.24) | copy-start | bytes 49156
  370.8 33.0 %copy-start.27 = (f32[1,32,128]{2,1,0:T(8,128)S(1)}, f32[1,32,128]{2,1,0:T(8,128)}, u32[]{:S(2)}) copy-start(f32[1,32,128]{2,1,0:T(8,128)} %copy-done.26) | copy-start | bytes 49156
  370.8 33.0 %copy-start.29 = (f32[1,32,128]{2,1,0:T(8,128)S(1)}, f32[1,32,128]{2,1,0:T(8,128)}, u32[]{:S(2)}) copy-start(f32[1,32,128]{2,1,0:T(8,128)} %copy-done.28) | copy-start | bytes 49156
  370.8 33.0 %copy-start.31 = (f32[1,32,128]{2,1,0:T(8,128)S(1)}, f32[1,32,128]{2,1,0:T(8,128)}, u32[]{:S(2)}) copy-start(f32[1,32,128]{2,1,0:T(8,128)} %copy-done.30) | copy-start | bytes 49156
  370.8 33.0 %copy-start.33 = (f32[1,32,128]{2,1,0:T(8,128)S(1)}, f32[1,32,128]{2,1,0:T(8,128)}, u32[]{:S(2)}) copy-start(f32[1,32,128]{2,1,0:T(8,128)} %copy-done.32) | copy-start | bytes 49156
  370.8 33.0 %copy-start.35 = (f32[1,32,128]{2,1,0:T(8,128)S(1)}, f32[1,32,128]{2,1,0:T(8,128)}, u32[]{:S(2)}) copy-start(f32[1,32,128]{2,1,0:T(8,128)} %copy-done.34) | copy-start | bytes 49156
  370.8 33.0 %copy-start.37 = (f32[1,32,128]{2,1,0:T(8,128)S(1)}, f32[1,32,128]{2,1,0:T(8,128)}, u32[]{:S(2)}) copy-start(f32[1,32,128]{2,1,0:T(8,128)} %copy-done.36) | copy-start | bytes 49156
  424.9 11.3 %collective-permute-start.4 = (f32[4,72,3,128]{3,1,2,0:T(8,128)S(1)}, f32[4,72,3,128]{3,1,2,0:T(8,128)S(1)}, u32[]{:S(2)}, u32[]{:S(2)}) collective-permute-start(f32[4,72,3,128]{3,1,2,0:T(8,128)S(1)} %copy.2504), channel_id=1, source_target_pairs={{8,0},{16,8},{24,16},{32,24},{40,32},{48,40},{56,48},{64,56},{72,6... | collective-permute-start | bytes 1327112 | tf_op jit(solution)/shard_map/ppermute | solution.py:22
  426.1 9.8 %collective-permute-start.5 = (f32[4,72,3,128]{3,1,2,0:T(8,128)S(1)}, f32[4,72,3,128]{3,1,2,0:T(8,128)S(1)}, u32[]{:S(2)}, u32[]{:S(2)}) collective-permute-start(f32[4,72,3,128]{3,1,2,0:T(8,128)S(1)} %copy.2507), channel_id=1, source_target_pairs={{0,8},{8,16},{16,24},{24,32},{32,40},{40,48},{48,56},{56,64},{64,7... | collective-permute-start | bytes 1327112 | tf_op jit(solution)/shard_map/ppermute | solution.py:20
  477.7 18.7 %collective-permute-start.7 = (f32[4,72,32,3]{1,2,3,0:T(8,128)S(1)}, f32[4,72,32,3]{1,2,3,0:T(8,128)S(1)}, u32[]{:S(2)}, u32[]{:S(2)}) collective-permute-start(f32[4,72,32,3]{1,2,3,0:T(8,128)S(1)} %copy.2520), channel_id=1, source_target_pairs={{0,1},{1,2},{2,3},{3,4},{4,5},{5,6},{6,7},{8,9},{9,10},{10,11},{11... | collective-permute-start | bytes 331784 | tf_op jit(solution)/shard_map/ppermute | solution.py:20
  483.6 18.0 %collective-permute-start.6 = (f32[4,72,32,3]{1,2,3,0:T(8,128)S(1)}, f32[4,72,32,3]{1,2,3,0:T(8,128)S(1)}, u32[]{:S(2)}, u32[]{:S(2)}) collective-permute-start(f32[4,72,32,3]{1,2,3,0:T(8,128)S(1)} %copy.2517), channel_id=1, source_target_pairs={{1,0},{2,1},{3,2},{4,3},{5,4},{6,5},{7,6},{9,8},{10,9},{11,10},{12... | collective-permute-start | bytes 331784 | tf_op jit(solution)/shard_map/ppermute | solution.py:22
  501.6 50.7 %slice-start = ((s8[4718592]{0:T(1024)(128)(4,1)}), s8[524288]{0:T(1024)(128)(4,1)S(1)}, s32[]{:S(2)}) async-start(s8[4718592]{0:T(1024)(128)(4,1)} %bitcast.3974), calls=%async_computation.2 | async-start | bytes 1048576
  506.6 45.7 %slice-start.1 = ((s8[4718592]{0:T(1024)(128)(4,1)}), s8[4194304]{0:T(1024)(128)(4,1)S(1)}, s32[]{:S(2)}) async-start(s8[4718592]{0:T(1024)(128)(4,1)} %bitcast.3974), calls=%async_computation.3 | async-start | bytes 8388608
  506.6 45.7 %copy-start.12 = (f32[72,32,128]{2,1,0:T(8,128)S(1)}, f32[72,32,128]{2,1,0:T(8,128)}, u32[]{:S(2)}) copy-start(f32[72,32,128]{2,1,0:T(8,128)} %multiply_multiply_fusion) | copy-start | bytes 3538948
  (199 other events, 2461.5 us)
